TPU v7x, 32 devices: a whole 2x2x4 slice. The times are simulated.
32 devices in a mesh: band: 2 (over y), row: 8 (over z, x), col: 2 (over core).
Axes of the slice: x: 2, y: 2, z: 4, core: 2. Of those that a mesh axis runs over, the one named last changes fastest.
Arguments:
- voltages: bfloat16 [4096, 161792], P(('band', 'row', 'col')), parts along dimension 0, may hold values from -6 to 6
- gains: float32 [4096, 32, 2], P(('band', 'row', 'col')), parts along dimension 0, may hold values from -4 to 4
Outputs:
- visibilities: bfloat16 [64, 2048, 2, 2048], P(('band', 'row'), None, None, 'col'), parts along dimension 0
There are 2 independent parts, one for each index of `band`. A program takes and returns all parts, laid end to end along the dimension named above; each array names one. Nothing has to cross between parts.
All inputs are finite; a program needn't handle non-finite values.
Results may differ from a plain program's by a relative error of at most 0.0075.
Values may be sent and summed in bfloat16 or wider, within the bound.
A program may use at most 192 MiB of HBM per device.

v0:
```python
import math

import jax
import jax.numpy as jnp
from jax import lax
from jax.sharding import PartitionSpec as P

FEEDS = 2048
NFFT = 2048
TAPS = 16
SPECTRA = 64


def prototype(taps, length):
    total = taps * length
    index = jnp.arange(total).astype(jnp.float32)
    offset = (index - (total - 1) / 2.0) / length
    window = 0.5 - 0.5 * jnp.cos(2.0 * math.pi * (index + 0.5) / total)
    return (jnp.sinc(offset) * window).reshape(taps, length)


def dft_table(length, chans, first):
    sample = jnp.arange(length)
    channel = first + jnp.arange(chans)
    phase = sample[:, None] * channel[None, :] % length
    angle = phase.astype(jnp.float32) * (2.0 * math.pi / length)
    return jnp.concatenate([jnp.cos(angle), -jnp.sin(angle)], axis=1).astype(jnp.bfloat16)


def shards(voltages, gains):
    rows = lax.axis_size("row")
    cols = lax.axis_size("col")
    feed_dev = voltages.shape[0]
    chans = gains.shape[1]
    sub = max(1, rows // chans)
    pairs = chans * sub // rows
    iblock = FEEDS // sub
    jblock = FEEDS // cols
    window = prototype(TAPS, NFFT)
    table = dft_table(NFFT, chans, NFFT // 8)
    scale = float(NFFT) ** (-0.5)
    blocks = voltages.reshape(feed_dev, -1, NFFT)
    total = jnp.zeros((feed_dev, SPECTRA, NFFT), jnp.float32)
    for tap in range(TAPS):
        total = total + blocks[:, tap : tap + SPECTRA, :].astype(jnp.float32) * window[tap]
    filtered = total.astype(jnp.bfloat16)
    raw = (
        jnp.dot(
            filtered.reshape(feed_dev * SPECTRA, NFFT), table, preferred_element_type=jnp.float32
        )
        * scale
    )
    raw = raw.reshape(feed_dev, SPECTRA, 2 * chans)
    real_part = raw[:, :, :chans]
    imag_part = raw[:, :, chans:]
    gain_re = gains[:, None, :, 0]
    gain_im = gains[:, None, :, 1]
    out_re = gain_re * real_part - gain_im * imag_part
    out_im = gain_re * imag_part + gain_im * real_part
    stacked = jnp.stack([out_re, out_im], axis=0)
    spectra = (
        jnp.transpose(stacked, (3, 1, 0, 2))
        .reshape(chans, feed_dev, 2 * SPECTRA)
        .astype(jnp.bfloat16)
    )
    outgoing = jnp.repeat(spectra, sub, axis=0)
    turned = lax.all_to_all(outgoing, "row", split_axis=0, concat_axis=1, tiled=True)
    turned = turned.reshape(pairs, rows, feed_dev, 2 * SPECTRA)
    gathered = lax.all_gather(turned, "col", axis=2, tiled=True)
    gathered = gathered.reshape(pairs, FEEDS, 2 * SPECTRA)
    pair_index = lax.axis_index("row") * pairs + jnp.arange(pairs)
    starts = pair_index % sub * iblock

    def first_rows(chan_rows, start):
        return lax.dynamic_slice_in_dim(chan_rows, start, iblock, 0)

    left = jax.vmap(first_rows)(gathered, starts)
    second = lax.dynamic_slice_in_dim(gathered, lax.axis_index("col") * jblock, jblock, 1)
    turned_second = jnp.concatenate([-second[:, :, SPECTRA:], second[:, :, :SPECTRA]], axis=2)
    right = jnp.concatenate([second, turned_second], axis=1)
    product = jnp.einsum("pis,pjs->pij", left, right, preferred_element_type=jnp.float32) / SPECTRA
    return product.astype(jnp.bfloat16).reshape(pairs, iblock, 2, jblock)


def solution(mesh):
    placed = (P(("band", "row", "col"), None), P(("band", "row", "col"), None, None))
    return jax.shard_map(
        shards,
        mesh=mesh,
        in_specs=placed,
        out_specs=P(("band", "row"), None, None, "col"),
        check_vma=False,
    )
```

profile of v0, /device:TPU:0, one launch (start us, length us, event | category | flops | bytes accessed | tf_op | source)
XLA Modules:
  0.0 479.6 jit_solution(14196050988857683254)
XLA Ops:
  6.5 0.6 fusion.20
  7.1 0.6 iota_add_fusion
  7.8 49.9 %copy.21 = bf16[128,161792]{0,1:T(8,128)(2,1)} copy(bf16[128,161792]{1,0:T(8,128)(2,1)} %param.2) | data formatting | bytes 82837504 | tf_op args[0]
  57.7 191.8 %add_convert_fusion = bf16[128,64,2048]{0,2,1:T(8,128)(2,1)} fusion(bf16[128,79,2048]{0,2,1:T(8,128)(2,1)} %bitcast.20, f32[2048]{0:T(1024)S(1)} %get-tuple-element.10, f32[2048]{0:T(1024)S(1)} %get-tuple-element.11, f32[2048]{0:T(1024)S(1)} %get-tuple-element.12, f32[2048]{0:T(1024)S(1)} %get-tuple-element.13, f32[2048]{0:T(1024)S(1)} %get-tuple-element.14, ...), kind=kLoop, calls=%fused_computation.2 | loop fusion | flops 805306368 | bytes 570556416 | tf_op jit(solution)/shard_map/convert_element_type | solution.py:46
  249.5 47.2 %copy.22 = bf16[128,64,2048]{2,1,0:T(8,128)(2,1)} copy(bf16[128,64,2048]{0,2,1:T(8,128)(2,1)} %add_convert_fusion) | data formatting | bytes 67108864 | tf_op jit(solution)/shard_map/convert_element_type | solution.py:46
  296.7 0.0 copy-done.1
  296.7 1.2 cosine_convert_fusion
  297.9 16.1 %convolution_multiply_fusion = f32[8192,64]{0,1:T(8,128)S(1)} fusion(bf16[8192,2048]{1,0:T(8,128)(2,1)} %bitcast.21, bf16[2048,32]{0,1:T(8,128)(2,1)S(1)} %get-tuple-element.28, bf16[2048,32]{0,1:T(8,128)(2,1)S(1)} %get-tuple-element.27), kind=kOutput, calls=%fused_computation.3 | convolution fusion | flops 2148532224 | bytes 35913728 | tf_op jit(solution)/shard_map/dot_general | solution.py:48
  314.0 3.0 reshape.78
  317.0 0.0 copy-done
  317.1 3.8 fusion.5
  320.9 0.5 maximum_bitcast_fusion
  321.3 0.9 copy.23
  322.3 32.8 %all_to_all.15 = bf16[32,128,128]{1,2,0:T(8,128)(2,1)S(1)} all-to-all(bf16[32,128,128]{1,2,0:T(8,128)(2,1)S(1)} %bitcast.26), channel_id=1, replica_groups=mesh['band'=2,'row'=8,'col'=2] {'row'}, dimensions={0} | all-to-all | bytes 2097152 | tf_op jit(solution)/shard_map/all_to_all | solution.py:67
  355.1 1.3 copy.24
  356.4 0.0 all-gather.2.cloned.1.call-update
  356.4 9.8 %all-gather.2.cloned.1.call-done = bf16[4,8,256,128]{3,2,0,1:T(8,128)(2,1)} async-done(((bf16[4,8,128,128]{3,2,0,1:T(8,128)(2,1)}), bf16[4,8,256,128]{3,2,0,1:T(8,128)(2,1)}) %all-gather.2.cloned.1.call-update) | async-done | bytes 2097168 | tf_op jit(solution)/shard_map/all_gather | solution.py:69
  366.2 1.7 copy.25
  367.9 2.6 copy.26
  370.5 1.1 constant_dynamic-slice_fusion.1
  371.6 1.5 dynamic-slice_negate_fusion
  373.2 2.3 gather_fusion
  375.5 15.5 %multiply_convert_fusion = bf16[4,2048,2048]{1,2,0:T(8,128)(2,1)} fusion(bf16[4,2048,128]{1,2,0:T(8,128)(2,1)S(1)} %gather_fusion, bf16[4,1024,64]{2,1,0:T(8,128)(2,1)} %get-tuple-element.8, bf16[4,1024,64]{2,1,0:T(8,128)(2,1)S(1)} %get-tuple-element.7, bf16[4,1024,128]{2,1,0:T(8,128)(2,1)} %constant_dynamic-slice_fusion.1), kind=kOutput, calls=%fused_computation.1 | convolution fusion | flops 4334813184 | bytes 37748736 | tf_op jit(solution)/shard_map/pis,pjs->pij/dot_general | solution.py:81
  391.0 81.8 %copy.28 = bf16[4,2048,2,1024]{3,2,1,0:T(2,128)(2,1)} copy(bf16[4,2048,2,1024]{1,3,2,0:T(8,128)(2,1)} %bitcast.22) | data formatting | bytes 67108864 | tf_op jit(solution)/shard_map/reshape | solution.py:82
  (6 shorter events, 0.0 us)
Async XLA Ops:
  6.5 359.7 %all-gather.2.cloned.1.call-start = ((), (), s32[]{:S(2)}) async-start(), calls=%async_computation.1 | async-start | bytes 3145728 | tf_op jit(solution)/shard_map/all_gather | solution.py:69
  249.5 47.2 %copy-start.1 = (s32[32]{0:T(128)S(1)}, s32[32]{0:T(128)}, u32[]{:S(2)}) copy-start(s32[32]{0:T(128)} %iota_add_fusion) | copy-start | bytes 388
  296.7 20.4 %copy-start = (f32[128,32,2]{0,2,1:T(2,128)S(1)}, f32[128,32,2]{0,2,1:T(2,128)}, u32[]{:S(2)}) copy-start(f32[128,32,2]{0,2,1:T(2,128)} %param.3) | copy-start | bytes 98308
Sparse Core Ops, SparseCore 0:
  356.5 9.6 all-gather.1
where the time goes:
time: 484 us; the launch traced here: 480 us
  other arithmetic  200 us (41%)
  local copies, waits for them, and re-layouts  192 us (40%)
  blocking collectives  32.8 us (7%)
  matrix products  31.6 us (7%)
  between operations  13.5 us (3%)
  waiting for transfers between devices  9.79 us (2%)
    convert_element_type x1, other arithmetic, shards(): filtered = total.astype(jnp.bfloat16)  192 us
    reshape x1, local copies, waits for them, and re-layouts, shards(): return product.astype(jnp.bfloat16).reshape(pairs, iblock, 2, jblock)  81.8 us
    unnamed x5, local copies, waits for them, and re-layouts  49.9 us
    convert_element_type x1, local copies, waits for them, and re-layouts, shards(): filtered = total.astype(jnp.bfloat16)  47.2 us
    all_to_all x1, blocking collectives, shards(): lax.all_to_all(outgoing, 'row', split_axis=0, concat_axis=1, tiled=True)  32.8 us
    dot_general x1, matrix products, shards(): jnp.dot(filtered.reshape(feed_dev * SPECTRA, NFFT), table, preferred_elem...  16.1 us
    dot_general x1, matrix products, shards(): jnp.einsum('pis,pjs->pij', left, right, preferred_element_type=jnp.float32)  15.5 us
    all_gather x1, waiting for transfers between devices, shards(): gathered = lax.all_gather(turned, 'col', axis=2, tiled=True)  9.77 us
  transfers between devices with their start and end apart: 1, of which 1 were waited for; matrix products, arithmetic and copies ran while one was open for 0% of the time, Pallas kernels for 0%

commit v1 on v0

--- a/solution.py
+++ b/solution.py
@@ -2,13 +2,21 @@
 
 import jax
 import jax.numpy as jnp
+import ml_dtypes
+import numpy as np
 from jax import lax
+from jax.experimental import pallas as pl
+from jax.experimental.pallas import tpu as pltpu
 from jax.sharding import PartitionSpec as P
 
 FEEDS = 2048
 NFFT = 2048
 TAPS = 16
 SPECTRA = 64
+LANES = 128
+STEP = 8
+MXU = 256
+MESH = pl.DeviceIdType.MESH
 
 
 def prototype(taps, length):
@@ -27,7 +35,7 @@
     return jnp.concatenate([jnp.cos(angle), -jnp.sin(angle)], axis=1).astype(jnp.bfloat16)
 
 
-def shards(voltages, gains):
+def plain_shards(voltages, gains):
     rows = lax.axis_size("row")
     cols = lax.axis_size("col")
     feed_dev = voltages.shape[0]
@@ -82,6 +90,334 @@
     return product.astype(jnp.bfloat16).reshape(pairs, iblock, 2, jblock)
 
 
+def folded_weights(chans, first):
+    total = TAPS * NFFT
+    m = np.arange(total)
+    h = np.sinc((m - (total - 1) / 2.0) / NFFT) * (
+        0.5 - 0.5 * np.cos(2.0 * np.pi * (m + 0.5) / total)
+    )
+    h = h.reshape(TAPS, NFFT)[:, : NFFT // 2]
+    n = np.arange(NFFT // 2) - (NFFT - 1) / 2.0
+    angle = 2.0 * np.pi / NFFT * n[:, None] * (first + np.arange(chans))[None, :]
+    cos, sin = np.cos(angle), np.sin(angle)
+    even, odd = [], []
+    for u in range(TAPS // 2):
+        plus = 0.5 * (h[u] + h[TAPS - 1 - u])[:, None]
+        minus = 0.5 * (h[u] - h[TAPS - 1 - u])[:, None]
+        even += [plus * cos, -minus * sin]
+        odd += [minus * cos, -plus * sin]
+    return [np.concatenate(x, axis=1).astype(ml_dtypes.bfloat16) for x in (even, odd)]
+
+
+def rotation(chans, first):
+    phase = -2.0 * np.pi / NFFT * (NFFT - 1) / 2.0 * (first + np.arange(chans))
+    scale = NFFT**-0.5 * SPECTRA**-0.5
+    turn = np.stack([np.cos(phase), np.sin(phase)], axis=1) * scale
+    return np.repeat(turn[:, :, None], LANES, axis=2).astype(np.float32)
+
+
+def channelize_kernel(rows, pairs, *refs):
+    frames = refs[:STEP]
+    even_w, odd_w, flip, gains, turn, out, even, odd, low_acc, high_acc, stage, ready = refs[STEP : STEP + 12]
+    send_sem, recv_sem, own_sem, pass_sem, passed_sem = refs[STEP + 12 :]
+    i = pl.program_id(0)
+    steps = pl.num_programs(0)
+    feed_dev = frames[0].shape[0]
+    half = NFFT // 2
+    band, row, col = lax.axis_index("band"), lax.axis_index("row"), lax.axis_index("col")
+    chunks = SPECTRA // STEP
+    chans = rows * pairs
+    delay = TAPS // STEP
+
+    def to_row(ch, d):
+        dest = lax.rem(row + d, rows)
+        return pltpu.make_async_remote_copy(
+            src_ref=ready.at[ch, pl.ds(dest * pairs, pairs)],
+            dst_ref=out.at[:, row, col, pl.ds(pl.multiple_of(ch * 2 * STEP, 2 * STEP), 2 * STEP), :],
+            send_sem=send_sem.at[ch, d],
+            recv_sem=recv_sem.at[ch, d],
+            device_id=(band, dest, col),
+            device_id_type=MESH,
+        )
+
+    def from_row(ch, d):
+        src = lax.rem(row + rows - d, rows)
+        return pltpu.make_async_remote_copy(
+            src_ref=ready.at[ch, pl.ds(src * pairs, pairs)],
+            dst_ref=out.at[:, src, col, pl.ds(pl.multiple_of(ch * 2 * STEP, 2 * STEP), 2 * STEP), :],
+            send_sem=send_sem.at[ch, d],
+            recv_sem=recv_sem.at[ch, d],
+            device_id=(band, src, col),
+            device_id_type=MESH,
+        )
+
+    def own(ch):
+        return pltpu.make_async_copy(
+            ready.at[ch, pl.ds(row * pairs, pairs)],
+            out.at[:, row, col, pl.ds(pl.multiple_of(ch * 2 * STEP, 2 * STEP), 2 * STEP), :],
+            own_sem.at[ch],
+        )
+
+    def to_sibling(ch, c):
+        block = out.at[:, :, c, pl.ds(pl.multiple_of(ch * 2 * STEP, 2 * STEP), 2 * STEP), :]
+        return pltpu.make_async_remote_copy(
+            src_ref=block,
+            dst_ref=block,
+            send_sem=pass_sem.at[ch],
+            recv_sem=passed_sem.at[ch],
+            device_id=(band, row, 1 - col),
+            device_id_type=MESH,
+        )
+
+    def hand_on(ch):
+        own(ch).wait()
+        for d in range(1, rows):
+            from_row(ch, d).wait_recv()
+        to_sibling(ch, col).start()
+
+    barrier = pltpu.get_barrier_semaphore()
+
+    @pl.when(i == 0)
+    def _():
+        for d in range(1, rows):
+            pl.semaphore_signal(
+                barrier, inc=1, device_id=(band, lax.rem(row + d, rows), col), device_id_type=MESH
+            )
+        pl.semaphore_signal(barrier, inc=1, device_id=(band, row, 1 - col), device_id_type=MESH)
+        low_acc[...] = jnp.zeros_like(low_acc)
+        high_acc[...] = jnp.zeros_like(high_acc)
+
+    for m in range(half // MXU):
+        tail = jnp.concatenate(
+            [f[:, NFFT - (m + 1) * MXU : NFFT - m * MXU] for f in frames], axis=0
+        )
+        tail = jnp.dot(tail, flip[...], preferred_element_type=jnp.float32).astype(jnp.bfloat16)
+        head = jnp.concatenate([f[:, m * MXU : (m + 1) * MXU] for f in frames], axis=0)
+        even[:, m * MXU : (m + 1) * MXU] = head + tail
+        odd[:, m * MXU : (m + 1) * MXU] = head - tail
+
+    for q in range(TAPS * chans // MXU):
+        ge = jnp.dot(even[...], even_w[:, q * MXU : (q + 1) * MXU], preferred_element_type=jnp.float32)
+        go = jnp.dot(odd[...], odd_w[:, q * MXU : (q + 1) * MXU], preferred_element_type=jnp.float32)
+        low = ge + go
+        high = ge - go
+        for t in range(MXU // LANES):
+            j = q * (MXU // LANES) + t
+            cut = slice(t * LANES, (t + 1) * LANES)
+            at = pl.ds(i * STEP + STEP - 2 - 2 * j, STEP)
+            low_acc[at] += low[:, cut].reshape(STEP, feed_dev, LANES)
+            at = pl.ds(i * STEP + 2 * j, STEP)
+            high_acc[at] += high[:, cut].reshape(STEP, feed_dev, LANES)
+
+    @pl.when(i == delay)
+    def _():
+        pl.semaphore_wait(barrier, rows)
+
+    @pl.when(i >= delay)
+    def _():
+        ch = i - delay
+        s0 = ch * STEP
+        lane = lax.broadcasted_iota(jnp.int32, (feed_dev, LANES), 1)
+        first = lane < LANES // 2
+        sign = jnp.where(lax.rem(lane, 2 * chans) < chans, 1.0, -1.0).astype(jnp.float32)
+        turn_re, turn_im = turn[:, 0, :], turn[:, 1, :]
+        own_re, own_im = gains[:, 0, :], gains[:, 1, :]
+        gain_re = own_re * turn_re - own_im * turn_im
+        gain_im = own_re * turn_im + own_im * turn_re
+        for s in range(0, STEP, 2):
+            a = [low_acc[s0 + STEP - 1 + s + e] + sign * high_acc[s0 + 2 * STEP + s + e] for e in (0, 1)]
+            b = [low_acc[s0 + STEP + s + e] + sign * high_acc[s0 + 2 * STEP - 1 + s + e] for e in (0, 1)]
+            mine = jnp.where(first, a[0], b[1])
+            other = jnp.where(first, a[1], b[0])
+            both = (mine + pltpu.roll(other, LANES // 2, 1)).T
+            for e in (0, 1):
+                re = both[2 * chans * e : 2 * chans * e + chans]
+                im = both[2 * chans * e + chans : 2 * chans * (e + 1)]
+                stage[pl.ds(s + e, chans, stride=2 * STEP), :] = gain_re * re - gain_im * im
+                stage[pl.ds(STEP + s + e, chans, stride=2 * STEP), :] = gain_re * im + gain_im * re
+        ready[ch] = stage[...].reshape(chans, 2 * STEP, LANES).astype(jnp.bfloat16)
+        for d in range(1, rows):
+            to_row(ch, d).start()
+        own(ch).start()
+
+    @pl.when(i >= 2 * delay)
+    def _():
+        hand_on(i - 2 * delay)
+
+    @pl.when(i == steps - 1)
+    def _():
+        for ch in range(chunks - delay, chunks):
+            hand_on(ch)
+
+        @pl.loop(0, chunks)
+        def _(ch):
+            for d in range(1, rows):
+                to_row(ch, d).wait_send()
+            to_sibling(ch, col).wait_send()
+            to_sibling(ch, 1 - col).wait_recv()
+
+
+def channelize(voltages, gains):
+    rows = lax.axis_size("row")
+    cols = lax.axis_size("col")
+    feed_dev, samples = voltages.shape
+    chans = gains.shape[1]
+    pairs = chans // rows
+    frames = samples // NFFT
+    steps = (frames + 1) // STEP
+    half = NFFT // 2
+    chunks = SPECTRA // STEP
+    even_w, odd_w = folded_weights(chans, NFFT // 8)
+    flip = np.eye(MXU)[::-1].astype(ml_dtypes.bfloat16)
+    turn = rotation(chans, NFFT // 8)
+
+    def frame_spec(a):
+        return pl.BlockSpec((feed_dev, NFFT), lambda i: (0, jnp.maximum(i * STEP + a - 1, 0)))
+
+    def whole(shape):
+        return pl.BlockSpec(shape, lambda i: (0,) * len(shape))
+
+    depth = steps * STEP + STEP
+
+    def kernel(*refs):
+        channelize_kernel(rows, pairs, *refs)
+
+    return pl.pallas_call(
+        kernel,
+        grid=(steps,),
+        out_shape=jax.ShapeDtypeStruct((pairs, rows, cols, 2 * SPECTRA, feed_dev), jnp.bfloat16),
+        in_specs=[frame_spec(a) for a in range(STEP)]
+        + [whole(even_w.shape), whole(odd_w.shape), whole(flip.shape)]
+        + [whole((chans, 2, feed_dev)), whole(turn.shape)],
+        out_specs=pl.BlockSpec(memory_space=pl.ANY),
+        scratch_shapes=[
+            pltpu.VMEM((STEP * feed_dev, half), jnp.bfloat16),
+            pltpu.VMEM((STEP * feed_dev, half), jnp.bfloat16),
+            pltpu.VMEM((depth, feed_dev, LANES), jnp.float32),
+            pltpu.VMEM((depth, feed_dev, LANES), jnp.float32),
+            pltpu.VMEM((chans * 2 * STEP, LANES), jnp.float32),
+            pltpu.VMEM((chunks, chans, 2 * STEP, LANES), jnp.bfloat16),
+            pltpu.SemaphoreType.DMA((chunks, rows)),
+            pltpu.SemaphoreType.DMA((chunks, rows)),
+            pltpu.SemaphoreType.DMA((chunks,)),
+            pltpu.SemaphoreType.DMA((chunks,)),
+            pltpu.SemaphoreType.DMA((chunks,)),
+        ],
+        compiler_params=pltpu.CompilerParams(
+            collective_id=0,
+            has_side_effects=True,
+            vmem_limit_bytes=56 << 20,
+            dimension_semantics=("arbitrary",),
+        ),
+        name="channelize",
+    )(
+        *([voltages] * STEP),
+        jnp.asarray(even_w),
+        jnp.asarray(odd_w),
+        jnp.asarray(flip),
+        jnp.transpose(gains, (1, 2, 0)),
+        jnp.asarray(turn),
+    )
+
+
+def correlate_kernel(spectra, out, mixed, held, sem):
+    _, rows, cols, depth, feed_dev = spectra.shape
+    c, q = pl.program_id(0), pl.program_id(1)
+    nq = pl.num_programs(1)
+    step = c * nq + q
+    last = pl.num_programs(0) * nq - 1
+    slot = lax.rem(step, 2)
+    parts = held.shape[1]
+    iblock = held.shape[2]
+    jblocks = rows * cols // lax.axis_size("col")
+    iblocks = iblock // feed_dev
+    col = lax.axis_index("col")
+
+    def put(st, jt):
+        return pltpu.make_async_copy(
+            held.at[lax.rem(st, 2), jt],
+            out.at[
+                lax.div(st, nq),
+                pl.ds(lax.rem(st, nq) * iblock, iblock),
+                :,
+                pl.ds(jt * LANES, LANES),
+            ],
+            sem.at[lax.rem(st, 2), jt],
+        )
+
+    for b in range(iblocks):
+        at = q * iblocks + b
+        y = spectra[0, lax.div(at, cols), lax.rem(at, cols)].astype(jnp.float32)
+        z = y.reshape(depth // (2 * STEP), 2, STEP, feed_dev)
+        z = jnp.concatenate([z[:, 1:], -z[:, :1]], axis=1).reshape(depth, feed_dev)
+        mixed[pl.ds(2 * b * feed_dev, feed_dev, stride=2), :] = y.T
+        mixed[pl.ds(2 * b * feed_dev + 1, feed_dev, stride=2), :] = z.T
+    left = mixed[...].astype(jnp.bfloat16)
+
+    @pl.when(step >= 2)
+    def _():
+        for jt in range(parts):
+            put(step - 2, jt).wait()
+
+    wide = MXU // LANES
+    for g in range(parts // wide):
+        side = []
+        for t in range(wide):
+            at = col * jblocks + g * wide + t
+            side.append(spectra[0, lax.div(at, cols), lax.rem(at, cols)])
+        right = jnp.concatenate(side, axis=1)
+        product = jnp.dot(left, right, preferred_element_type=jnp.float32).astype(jnp.bfloat16)
+        for t in range(wide):
+            jt = g * wide + t
+            held.at[slot, jt].reshape(2 * iblock, LANES)[...] = product[:, t * LANES : (t + 1) * LANES]
+            put(step, jt).start()
+
+    @pl.when(step == last)
+    def _():
+        for st in (last - 1, last):
+            for jt in range(parts):
+                put(st, jt).wait()
+
+
+def correlate(spectra):
+    pairs, rows, cols, depth, feed_dev = spectra.shape
+    jblock = FEEDS // cols
+    iblock = 4 * feed_dev
+    return pl.pallas_call(
+        correlate_kernel,
+        grid=(pairs, FEEDS // iblock),
+        out_shape=jax.ShapeDtypeStruct((pairs, FEEDS, 2, jblock), jnp.bfloat16),
+        in_specs=[pl.BlockSpec((1, rows, cols, depth, feed_dev), lambda c, q: (c, 0, 0, 0, 0))],
+        out_specs=pl.BlockSpec(memory_space=pl.ANY),
+        scratch_shapes=[
+            pltpu.VMEM((2 * iblock, depth), jnp.float32),
+            pltpu.VMEM((2, jblock // LANES, iblock, 2, LANES), jnp.bfloat16),
+            pltpu.SemaphoreType.DMA((2, jblock // LANES)),
+        ],
+        compiler_params=pltpu.CompilerParams(
+            vmem_limit_bytes=40 << 20, dimension_semantics=("arbitrary", "arbitrary")
+        ),
+        name="correlate",
+    )(spectra)
+
+
+def shards(voltages, gains):
+    rows = lax.axis_size("row")
+    cols = lax.axis_size("col")
+    chans = gains.shape[1]
+    fits = (
+        voltages.shape[0] == LANES
+        and rows * cols * LANES == FEEDS
+        and cols == 2
+        and chans % rows == 0
+        and 4 * chans == LANES
+        and voltages.shape[1] == (SPECTRA + TAPS - 1) * NFFT
+    )
+    if not fits:
+        return plain_shards(voltages, gains)
+    return correlate(channelize(voltages, gains))
+
+
 def solution(mesh):
     placed = (P(("band", "row", "col"), None), P(("band", "row", "col"), None, None))
     return jax.shard_map(

time: 484 us -> 93.9 us (0.19)
  other arithmetic: 200 us -> 0 us
  local copies, waits for them, and re-layouts: 192 us -> 1.58 us
  Pallas kernels: 0 us -> 92.2 us
  blocking collectives: 32.8 us -> 0 us
  matrix products: 31.6 us -> 0 us
  between operations: 13.5 us -> 0.02 us
  waiting for transfers between devices: 9.79 us -> 0 us
    convert_element_type x2 -> x0, other arithmetic: 192 us -> none  [the longest x1 192 us: shards(): filtered = total.astype(jnp.bfloat16)]
    pallas_call x0 -> x2, Pallas kernels: none -> 92.2 us  [the longest x1 48 us: channelize(): pl.pallas_call(kernel, grid=(steps,), out_shape=jax.ShapeDtypeStruct((pai...]
    reshape x3 -> x0, local copies, waits for them, and re-layouts: 87.4 us -> none  [the longest x1 81.8 us: shards(): return product.astype(jnp.bfloat16).reshape(pairs, iblock, 2, jblock)]
    unnamed x5 -> x2, local copies, waits for them, and re-layouts: 49.9 us -> 1.58 us
    convert_element_type x2 -> x0, local copies, waits for them, and re-layouts: 48.1 us -> none  [the longest x1 47.2 us: shards(): filtered = total.astype(jnp.bfloat16)]
    all_to_all x1 -> x0, blocking collectives: 32.8 us -> none  [shards(): lax.all_to_all(outgoing, 'row', split_axis=0, concat_axis=1, tiled=True)]
    dot_general x2 -> x0, matrix products: 31.6 us -> none  [the longest x1 16.1 us: shards(): jnp.dot(filtered.reshape(feed_dev * SPECTRA, NFFT), table, preferred_elem...]
    all_gather x1 -> x0, waiting for transfers between devices: 9.77 us -> none  [shards(): gathered = lax.all_gather(turned, 'col', axis=2, tiled=True)]
  transfers between devices with their start and end apart: 1 -> 0, of which waited for: 1 -> 0; matrix products, arithmetic and copies ran while one was open for 0% -> 0% of each run, Pallas kernels for 0% -> 0%
where the time goes in v1:
time: 93.9 us; the launch traced here: 93.8 us
  Pallas kernels  92.2 us (98%)
  local copies, waits for them, and re-layouts  1.58 us (2%)
    pallas_call x1, Pallas kernels, channelize(): pl.pallas_call(kernel, grid=(steps,), out_shape=jax.ShapeDtypeStruct((pai...  48 us
    pallas_call x1, Pallas kernels, correlate(): pl.pallas_call(correlate_kernel, grid=(pairs, FEEDS // iblock), out_shape...  44.2 us

profile of v1, /device:TPU:0, one launch (start us, length us, event | category | flops | bytes accessed | tf_op | source)
XLA Modules:
  0.0 93.8 jit_solution(16221500704135751043)
XLA Ops:
  0.0 48.0 %channelize.1.spectra = bf16[4,8,2,128,128]{4,3,2,1,0:T(8,128)(2,1)} custom-call(bf16[128,161792]{1,0:T(8,128)(2,1)} %refs_7_.1, bf16[128,161792]{1,0:T(8,128)(2,1)} %refs_7_.1, bf16[128,161792]{1,0:T(8,128)(2,1)} %refs_7_.1, bf16[128,161792]{1,0:T(8,128)(2,1)} %refs_7_.1, bf16[128,161792]{1,0:T(8,128)(2,1)} %refs_7_.1, bf16[128,161792]{1,0:T(8,128)(2,1)} %refs_7_.1, ...), custom_call_target="tpu_custom_call" | custom-call | tf_op jit(solution)/shard_map/channelize/pallas_call | solution.py:285
  48.0 0.0 copy-start
  48.0 1.6 %copy-done = bf16[4,8,2,128,128]{4,3,2,1,0:T(8,128)(2,1)S(1)} copy-done((bf16[4,8,2,128,128]{4,3,2,1,0:T(8,128)(2,1)S(1)}, bf16[4,8,2,128,128]{4,3,2,1,0:T(8,128)(2,1)}, u32[]{:S(2)}) %copy-start) | copy-done | bytes 2097176
  49.6 44.2 %correlate.1 = bf16[4,2048,2,1024]{3,2,1,0:T(2,128)(2,1)} custom-call(bf16[4,8,2,128,128]{4,3,2,1,0:T(8,128)(2,1)S(1)} %copy-done), custom_call_target="tpu_custom_call" | custom-call | tf_op jit(solution)/shard_map/correlate/pallas_call | solution.py:386
Async XLA Ops:
  48.0 1.6 %copy-start = (bf16[4,8,2,128,128]{4,3,2,1,0:T(8,128)(2,1)S(1)}, bf16[4,8,2,128,128]{4,3,2,1,0:T(8,128)(2,1)}, u32[]{:S(2)}) copy-start(bf16[4,8,2,128,128]{4,3,2,1,0:T(8,128)(2,1)} %channelize.1.spectra) | copy-start | bytes 6291460

commit v2 on v1

--- a/solution.py
+++ b/solution.py
@@ -15,7 +15,9 @@
 SPECTRA = 64
 LANES = 128
 STEP = 8
+GROUP = 2
 MXU = 256
+PITCH = 17
 MESH = pl.DeviceIdType.MESH
 
 
@@ -187,27 +189,33 @@
         low_acc[...] = jnp.zeros_like(low_acc)
         high_acc[...] = jnp.zeros_like(high_acc)
 
-    for m in range(half // MXU):
-        tail = jnp.concatenate(
-            [f[:, NFFT - (m + 1) * MXU : NFFT - m * MXU] for f in frames], axis=0
-        )
-        tail = jnp.dot(tail, flip[...], preferred_element_type=jnp.float32).astype(jnp.bfloat16)
-        head = jnp.concatenate([f[:, m * MXU : (m + 1) * MXU] for f in frames], axis=0)
-        even[:, m * MXU : (m + 1) * MXU] = head + tail
-        odd[:, m * MXU : (m + 1) * MXU] = head - tail
-
-    for q in range(TAPS * chans // MXU):
-        ge = jnp.dot(even[...], even_w[:, q * MXU : (q + 1) * MXU], preferred_element_type=jnp.float32)
-        go = jnp.dot(odd[...], odd_w[:, q * MXU : (q + 1) * MXU], preferred_element_type=jnp.float32)
-        low = ge + go
-        high = ge - go
-        for t in range(MXU // LANES):
-            j = q * (MXU // LANES) + t
-            cut = slice(t * LANES, (t + 1) * LANES)
-            at = pl.ds(i * STEP + STEP - 2 - 2 * j, STEP)
-            low_acc[at] += low[:, cut].reshape(STEP, feed_dev, LANES)
-            at = pl.ds(i * STEP + 2 * j, STEP)
-            high_acc[at] += high[:, cut].reshape(STEP, feed_dev, LANES)
+    for first in range(0, STEP, GROUP):
+        group = frames[first : first + GROUP]
+        span = slice(first * feed_dev, (first + GROUP) * feed_dev)
+        for m in range(half // MXU):
+            tail = jnp.concatenate(
+                [f[:, NFFT - (m + 1) * MXU : NFFT - m * MXU] for f in group], axis=0
+            )
+            tail = jnp.dot(tail, flip[...], preferred_element_type=jnp.float32).astype(jnp.bfloat16)
+            head = jnp.concatenate([f[:, m * MXU : (m + 1) * MXU] for f in group], axis=0)
+            even[span, m * MXU : (m + 1) * MXU] = head + tail
+            odd[span, m * MXU : (m + 1) * MXU] = head - tail
+
+    for first in range(0, STEP, GROUP):
+        span = slice(first * feed_dev, (first + GROUP) * feed_dev)
+        for q in range(TAPS * chans // MXU):
+            cols = slice(q * MXU, (q + 1) * MXU)
+            ge = jnp.dot(even[span], even_w[:, cols], preferred_element_type=jnp.float32)
+            go = jnp.dot(odd[span], odd_w[:, cols], preferred_element_type=jnp.float32)
+            low = ge + go
+            high = ge - go
+            for t in range(MXU // LANES):
+                j = q * (MXU // LANES) + t
+                cut = slice(t * LANES, (t + 1) * LANES)
+                at = pl.ds(i * STEP + STEP - 2 - 2 * j + first, GROUP)
+                low_acc[at] += low[:, cut].reshape(GROUP, feed_dev, LANES)
+                at = pl.ds(i * STEP + 2 * j + first, GROUP)
+                high_acc[at] += high[:, cut].reshape(GROUP, feed_dev, LANES)
 
     @pl.when(i == delay)
     def _():
@@ -320,44 +328,24 @@
     )
 
 
-def correlate_kernel(spectra, out, mixed, held, sem):
+def correlate_kernel(spectra, out, wide_rows):
     _, rows, cols, depth, feed_dev = spectra.shape
-    c, q = pl.program_id(0), pl.program_id(1)
-    nq = pl.num_programs(1)
-    step = c * nq + q
-    last = pl.num_programs(0) * nq - 1
-    slot = lax.rem(step, 2)
-    parts = held.shape[1]
-    iblock = held.shape[2]
+    q = pl.program_id(1)
+    iblock = wide_rows.shape[0] // PITCH
+    parts = out.shape[1] // iblock // 2
     jblocks = rows * cols // lax.axis_size("col")
     iblocks = iblock // feed_dev
     col = lax.axis_index("col")
 
-    def put(st, jt):
-        return pltpu.make_async_copy(
-            held.at[lax.rem(st, 2), jt],
-            out.at[
-                lax.div(st, nq),
-                pl.ds(lax.rem(st, nq) * iblock, iblock),
-                :,
-                pl.ds(jt * LANES, LANES),
-            ],
-            sem.at[lax.rem(st, 2), jt],
-        )
-
+    re_side, im_side = [], []
     for b in range(iblocks):
         at = q * iblocks + b
         y = spectra[0, lax.div(at, cols), lax.rem(at, cols)].astype(jnp.float32)
         z = y.reshape(depth // (2 * STEP), 2, STEP, feed_dev)
         z = jnp.concatenate([z[:, 1:], -z[:, :1]], axis=1).reshape(depth, feed_dev)
-        mixed[pl.ds(2 * b * feed_dev, feed_dev, stride=2), :] = y.T
-        mixed[pl.ds(2 * b * feed_dev + 1, feed_dev, stride=2), :] = z.T
-    left = mixed[...].astype(jnp.bfloat16)
-
-    @pl.when(step >= 2)
-    def _():
-        for jt in range(parts):
-            put(step - 2, jt).wait()
+        re_side.append(y.T.astype(jnp.bfloat16))
+        im_side.append(z.T.astype(jnp.bfloat16))
+    lefts = [jnp.concatenate(x, axis=0) for x in (re_side, im_side)]
 
     wide = MXU // LANES
     for g in range(parts // wide):
@@ -366,39 +354,37 @@
             at = col * jblocks + g * wide + t
             side.append(spectra[0, lax.div(at, cols), lax.rem(at, cols)])
         right = jnp.concatenate(side, axis=1)
-        product = jnp.dot(left, right, preferred_element_type=jnp.float32).astype(jnp.bfloat16)
-        for t in range(wide):
-            jt = g * wide + t
-            held.at[slot, jt].reshape(2 * iblock, LANES)[...] = product[:, t * LANES : (t + 1) * LANES]
-            put(step, jt).start()
-
-    @pl.when(step == last)
-    def _():
-        for st in (last - 1, last):
-            for jt in range(parts):
-                put(st, jt).wait()
+        for p in (0, 1):
+            product = jnp.dot(lefts[p], right, preferred_element_type=jnp.float32)
+            for t in range(wide):
+                at = 2 * (g * wide + t) + p
+                wide_rows[pl.ds(at, iblock, stride=PITCH), :] = product[:, t * LANES : (t + 1) * LANES]
+
+    @pl.loop(0, iblock, unroll=16)
+    def _(r):
+        rows_of = wide_rows[pl.ds(r * PITCH, 2 * parts), :]
+        out[0, pl.ds(pl.multiple_of(r * 2 * parts, 2 * parts), 2 * parts), :] = rows_of.astype(jnp.bfloat16)
 
 
 def correlate(spectra):
     pairs, rows, cols, depth, feed_dev = spectra.shape
     jblock = FEEDS // cols
     iblock = 4 * feed_dev
-    return pl.pallas_call(
+    parts = jblock // LANES
+    flat = pl.pallas_call(
         correlate_kernel,
         grid=(pairs, FEEDS // iblock),
-        out_shape=jax.ShapeDtypeStruct((pairs, FEEDS, 2, jblock), jnp.bfloat16),
+        out_shape=jax.ShapeDtypeStruct((pairs, FEEDS * 2 * parts, LANES), jnp.bfloat16),
         in_specs=[pl.BlockSpec((1, rows, cols, depth, feed_dev), lambda c, q: (c, 0, 0, 0, 0))],
-        out_specs=pl.BlockSpec(memory_space=pl.ANY),
-        scratch_shapes=[
-            pltpu.VMEM((2 * iblock, depth), jnp.float32),
-            pltpu.VMEM((2, jblock // LANES, iblock, 2, LANES), jnp.bfloat16),
-            pltpu.SemaphoreType.DMA((2, jblock // LANES)),
-        ],
+        out_specs=pl.BlockSpec((1, iblock * 2 * parts, LANES), lambda c, q: (c, q, 0)),
+        scratch_shapes=[pltpu.VMEM((iblock * PITCH, LANES), jnp.float32)],
         compiler_params=pltpu.CompilerParams(
-            vmem_limit_bytes=40 << 20, dimension_semantics=("arbitrary", "arbitrary")
+            vmem_limit_bytes=63 << 20, dimension_semantics=("arbitrary", "arbitrary")
         ),
         name="correlate",
     )(spectra)
+    flat = flat.reshape(pairs, FEEDS, parts, 2, LANES)
+    return jnp.transpose(flat, (0, 1, 3, 2, 4)).reshape(pairs, FEEDS, 2, jblock)
 
 
 def shards(voltages, gains):
@@ -409,6 +395,7 @@
         voltages.shape[0] == LANES
         and rows * cols * LANES == FEEDS
         and cols == 2
+        and FEEDS // cols // LANES == 8
         and chans % rows == 0
         and 4 * chans == LANES
         and voltages.shape[1] == (SPECTRA + TAPS - 1) * NFFT

time: 93.9 us -> 74.9 us (0.80)
  Pallas kernels: 92.2 us -> 74.8 us
  local copies, waits for them, and re-layouts: 1.58 us -> 0 us
    pallas_call x1, Pallas kernels: 44.2 us -> 26.5 us  [correlate(): pl.pallas_call(correlate_kernel, grid=(pairs, FEEDS // iblock), out_shape...]
    unnamed x2 -> x0, local copies, waits for them, and re-layouts: 1.58 us -> none
where the time goes in v2:
time: 74.9 us; the launch traced here: 74.8 us
  Pallas kernels  74.8 us (100%)
    pallas_call x1, Pallas kernels, channelize(): pl.pallas_call(kernel, grid=(steps,), out_shape=jax.ShapeDtypeStruct((pai...  48.3 us
    pallas_call x1, Pallas kernels, correlate(): pl.pallas_call(correlate_kernel, grid=(pairs, FEEDS // iblock), out_shape...  26.5 us

profile of v2, /device:TPU:0, one launch (start us, length us, event | category | flops | bytes accessed | tf_op | source)
XLA Modules:
  0.0 74.8 jit_solution(8314238492967137926)
XLA Ops:
  0.0 48.3 %channelize.1.spectra = bf16[4,8,2,128,128]{4,3,2,1,0:T(8,128)(2,1)} custom-call(bf16[128,161792]{1,0:T(8,128)(2,1)} %refs_7_.1, bf16[128,161792]{1,0:T(8,128)(2,1)} %refs_7_.1, bf16[128,161792]{1,0:T(8,128)(2,1)} %refs_7_.1, bf16[128,161792]{1,0:T(8,128)(2,1)} %refs_7_.1, bf16[128,161792]{1,0:T(8,128)(2,1)} %refs_7_.1, bf16[128,161792]{1,0:T(8,128)(2,1)} %refs_7_.1, ...), custom_call_target="tpu_custom_call" | custom-call | tf_op jit(solution)/shard_map/channelize/pallas_call | solution.py:293
  48.3 26.5 %correlate.1 = bf16[4,32768,128]{2,1,0:T(8,128)(2,1)} custom-call(bf16[4,8,2,128,128]{4,3,2,1,0:T(8,128)(2,1)} %channelize.1.spectra), custom_call_target="tpu_custom_call" | custom-call | tf_op jit(solution)/shard_map/correlate/pallas_call | solution.py:374

commit v3 on v2

--- a/solution.py
+++ b/solution.py
@@ -120,8 +120,8 @@
 
 def channelize_kernel(rows, pairs, *refs):
     frames = refs[:STEP]
-    even_w, odd_w, flip, gains, turn, out, even, odd, low_acc, high_acc, stage, ready = refs[STEP : STEP + 12]
-    send_sem, recv_sem, own_sem, pass_sem, passed_sem = refs[STEP + 12 :]
+    even_w, odd_w, gains, turn, out, even, odd, low_acc, high_acc, stage, ready = refs[STEP : STEP + 11]
+    send_sem, recv_sem, own_sem, pass_sem, passed_sem = refs[STEP + 11 :]
     i = pl.program_id(0)
     steps = pl.num_programs(0)
     feed_dev = frames[0].shape[0]
@@ -189,17 +189,19 @@
         low_acc[...] = jnp.zeros_like(low_acc)
         high_acc[...] = jnp.zeros_like(high_acc)
 
+    back = LANES - 1 - lax.broadcasted_iota(jnp.int32, (GROUP * feed_dev, LANES), 1)
     for first in range(0, STEP, GROUP):
         group = frames[first : first + GROUP]
         span = slice(first * feed_dev, (first + GROUP) * feed_dev)
-        for m in range(half // MXU):
+        for m in range(half // LANES):
             tail = jnp.concatenate(
-                [f[:, NFFT - (m + 1) * MXU : NFFT - m * MXU] for f in group], axis=0
-            )
-            tail = jnp.dot(tail, flip[...], preferred_element_type=jnp.float32).astype(jnp.bfloat16)
-            head = jnp.concatenate([f[:, m * MXU : (m + 1) * MXU] for f in group], axis=0)
-            even[span, m * MXU : (m + 1) * MXU] = head + tail
-            odd[span, m * MXU : (m + 1) * MXU] = head - tail
+                [f[:, NFFT - (m + 1) * LANES : NFFT - m * LANES] for f in group], axis=0
+            ).astype(jnp.float32)
+            tail = jnp.take_along_axis(tail, back, axis=1, mode="promise_in_bounds")
+            tail = tail.astype(jnp.bfloat16)
+            head = jnp.concatenate([f[:, m * LANES : (m + 1) * LANES] for f in group], axis=0)
+            even[span, m * LANES : (m + 1) * LANES] = head + tail
+            odd[span, m * LANES : (m + 1) * LANES] = head - tail
 
     for first in range(0, STEP, GROUP):
         span = slice(first * feed_dev, (first + GROUP) * feed_dev)
@@ -276,7 +278,6 @@
     half = NFFT // 2
     chunks = SPECTRA // STEP
     even_w, odd_w = folded_weights(chans, NFFT // 8)
-    flip = np.eye(MXU)[::-1].astype(ml_dtypes.bfloat16)
     turn = rotation(chans, NFFT // 8)
 
     def frame_spec(a):
@@ -295,7 +296,7 @@
         grid=(steps,),
         out_shape=jax.ShapeDtypeStruct((pairs, rows, cols, 2 * SPECTRA, feed_dev), jnp.bfloat16),
         in_specs=[frame_spec(a) for a in range(STEP)]
-        + [whole(even_w.shape), whole(odd_w.shape), whole(flip.shape)]
+        + [whole(even_w.shape), whole(odd_w.shape)]
         + [whole((chans, 2, feed_dev)), whole(turn.shape)],
         out_specs=pl.BlockSpec(memory_space=pl.ANY),
         scratch_shapes=[
@@ -322,7 +323,6 @@
         *([voltages] * STEP),
         jnp.asarray(even_w),
         jnp.asarray(odd_w),
-        jnp.asarray(flip),
         jnp.transpose(gains, (1, 2, 0)),
         jnp.asarray(turn),
     )
@@ -330,40 +330,45 @@
 
 def correlate_kernel(spectra, out, wide_rows):
     _, rows, cols, depth, feed_dev = spectra.shape
-    q = pl.program_id(1)
-    iblock = wide_rows.shape[0] // PITCH
+    nq = FEEDS // (wide_rows.shape[1] // PITCH)
+    step = jnp.minimum(pl.program_id(0), pl.num_programs(0) - 2)
+    q = lax.rem(step, nq)
+    slot = lax.rem(pl.program_id(0), 2)
+    iblock = wide_rows.shape[1] // PITCH
     parts = out.shape[1] // iblock // 2
     jblocks = rows * cols // lax.axis_size("col")
     iblocks = iblock // feed_dev
     col = lax.axis_index("col")
-
-    re_side, im_side = [], []
+    wide = MXU // LANES
+
+    lefts = []
     for b in range(iblocks):
         at = q * iblocks + b
         y = spectra[0, lax.div(at, cols), lax.rem(at, cols)].astype(jnp.float32)
         z = y.reshape(depth // (2 * STEP), 2, STEP, feed_dev)
         z = jnp.concatenate([z[:, 1:], -z[:, :1]], axis=1).reshape(depth, feed_dev)
-        re_side.append(y.T.astype(jnp.bfloat16))
-        im_side.append(z.T.astype(jnp.bfloat16))
-    lefts = [jnp.concatenate(x, axis=0) for x in (re_side, im_side)]
-
-    wide = MXU // LANES
+        lefts.append([y.T.astype(jnp.bfloat16), z.T.astype(jnp.bfloat16)])
+    lefts = [jnp.concatenate(x, axis=0) for x in zip(*lefts)]
+    rights = []
     for g in range(parts // wide):
         side = []
         for t in range(wide):
             at = col * jblocks + g * wide + t
             side.append(spectra[0, lax.div(at, cols), lax.rem(at, cols)])
-        right = jnp.concatenate(side, axis=1)
+        rights.append(jnp.concatenate(side, axis=1))
+
+    pieces = 2 * (parts // wide)
+    share = iblock // pieces
+    for g in range(parts // wide):
         for p in (0, 1):
-            product = jnp.dot(lefts[p], right, preferred_element_type=jnp.float32)
+            product = jnp.dot(lefts[p], rights[g], preferred_element_type=jnp.float32)
             for t in range(wide):
                 at = 2 * (g * wide + t) + p
-                wide_rows[pl.ds(at, iblock, stride=PITCH), :] = product[:, t * LANES : (t + 1) * LANES]
-
-    @pl.loop(0, iblock, unroll=16)
-    def _(r):
-        rows_of = wide_rows[pl.ds(r * PITCH, 2 * parts), :]
-        out[0, pl.ds(pl.multiple_of(r * 2 * parts, 2 * parts), 2 * parts), :] = rows_of.astype(jnp.bfloat16)
+                cut = product[:, t * LANES : (t + 1) * LANES]
+                wide_rows[slot, pl.ds(at, iblock, stride=PITCH), :] = cut
+            for r in range((2 * g + p) * share, (2 * g + p + 1) * share):
+                rows_of = wide_rows[1 - slot, pl.ds(r * PITCH + lax.div(q, nq), 2 * parts), :]
+                out[0, r * 2 * parts : (r + 1) * 2 * parts, :] = rows_of.astype(jnp.bfloat16)
 
 
 def correlate(spectra):
@@ -371,15 +376,25 @@
     jblock = FEEDS // cols
     iblock = 4 * feed_dev
     parts = jblock // LANES
+    nq = FEEDS // iblock
+    steps = pairs * nq
+
+    def taken(n):
+        return (jnp.minimum(n, steps - 1) // nq, 0, 0, 0, 0)
+
+    def given(n):
+        before = jnp.maximum(n - 1, 0)
+        return (before // nq, before % nq, 0)
+
     flat = pl.pallas_call(
         correlate_kernel,
-        grid=(pairs, FEEDS // iblock),
+        grid=(steps + 1,),
         out_shape=jax.ShapeDtypeStruct((pairs, FEEDS * 2 * parts, LANES), jnp.bfloat16),
-        in_specs=[pl.BlockSpec((1, rows, cols, depth, feed_dev), lambda c, q: (c, 0, 0, 0, 0))],
-        out_specs=pl.BlockSpec((1, iblock * 2 * parts, LANES), lambda c, q: (c, q, 0)),
-        scratch_shapes=[pltpu.VMEM((iblock * PITCH, LANES), jnp.float32)],
+        in_specs=[pl.BlockSpec((1, rows, cols, depth, feed_dev), taken)],
+        out_specs=pl.BlockSpec((1, iblock * 2 * parts, LANES), given),
+        scratch_shapes=[pltpu.VMEM((2, iblock * PITCH, LANES), jnp.float32)],
         compiler_params=pltpu.CompilerParams(
-            vmem_limit_bytes=63 << 20, dimension_semantics=("arbitrary", "arbitrary")
+            vmem_limit_bytes=63 << 20, dimension_semantics=("arbitrary",)
         ),
         name="correlate",
     )(spectra)

time: 74.9 us -> 71.4 us (0.953)
  Pallas kernels: 74.8 us -> 71.1 us
    pallas_call x1, Pallas kernels: 26.5 us -> 22.4 us  [correlate(): pl.pallas_call(correlate_kernel, grid=(steps + 1,), out_shape=jax.ShapeDt...]
where the time goes in v3:
time: 71.4 us; the launch traced here: 71.1 us
  Pallas kernels  71.1 us (100%)
    pallas_call x1, Pallas kernels, channelize(): pl.pallas_call(kernel, grid=(steps,), out_shape=jax.ShapeDtypeStruct((pai...  48.8 us
    pallas_call x1, Pallas kernels, correlate(): pl.pallas_call(correlate_kernel, grid=(steps + 1,), out_shape=jax.ShapeDt...  22.4 us

profile of v3, /device:TPU:0, one launch (start us, length us, event | category | flops | bytes accessed | tf_op | source)
XLA Modules:
  0.0 71.1 jit_solution(4459560455988472731)
XLA Ops:
  0.0 48.8 %channelize.1.spectra = bf16[4,8,2,128,128]{4,3,2,1,0:T(8,128)(2,1)} custom-call(bf16[128,161792]{1,0:T(8,128)(2,1)} %refs_7_.1, bf16[128,161792]{1,0:T(8,128)(2,1)} %refs_7_.1, bf16[128,161792]{1,0:T(8,128)(2,1)} %refs_7_.1, bf16[128,161792]{1,0:T(8,128)(2,1)} %refs_7_.1, bf16[128,161792]{1,0:T(8,128)(2,1)} %refs_7_.1, bf16[128,161792]{1,0:T(8,128)(2,1)} %refs_7_.1, ...), custom_call_target="tpu_custom_call" | custom-call | tf_op jit(solution)/shard_map/channelize/pallas_call | solution.py:294
  48.8 22.4 %correlate.1 = bf16[4,32768,128]{2,1,0:T(8,128)(2,1)} custom-call(bf16[4,8,2,128,128]{4,3,2,1,0:T(8,128)(2,1)} %channelize.1.spectra), custom_call_target="tpu_custom_call" | custom-call | tf_op jit(solution)/shard_map/correlate/pallas_call | solution.py:389

commit v4 on v3

--- a/solution.py
+++ b/solution.py
@@ -16,6 +16,7 @@
 LANES = 128
 STEP = 8
 GROUP = 2
+LAG = 3
 MXU = 256
 PITCH = 17
 MESH = pl.DeviceIdType.MESH
@@ -190,7 +191,8 @@
         high_acc[...] = jnp.zeros_like(high_acc)
 
     back = LANES - 1 - lax.broadcasted_iota(jnp.int32, (GROUP * feed_dev, LANES), 1)
-    for first in range(0, STEP, GROUP):
+
+    def fold(first):
         group = frames[first : first + GROUP]
         span = slice(first * feed_dev, (first + GROUP) * feed_dev)
         for m in range(half // LANES):
@@ -203,12 +205,15 @@
             even[span, m * LANES : (m + 1) * LANES] = head + tail
             odd[span, m * LANES : (m + 1) * LANES] = head - tail
 
+    fold(0)
     for first in range(0, STEP, GROUP):
         span = slice(first * feed_dev, (first + GROUP) * feed_dev)
         for q in range(TAPS * chans // MXU):
             cols = slice(q * MXU, (q + 1) * MXU)
             ge = jnp.dot(even[span], even_w[:, cols], preferred_element_type=jnp.float32)
             go = jnp.dot(odd[span], odd_w[:, cols], preferred_element_type=jnp.float32)
+            if q == 0 and first + GROUP < STEP:
+                fold(first + GROUP)
             low = ge + go
             high = ge - go
             for t in range(MXU // LANES):
@@ -246,17 +251,17 @@
                 stage[pl.ds(s + e, chans, stride=2 * STEP), :] = gain_re * re - gain_im * im
                 stage[pl.ds(STEP + s + e, chans, stride=2 * STEP), :] = gain_re * im + gain_im * re
         ready[ch] = stage[...].reshape(chans, 2 * STEP, LANES).astype(jnp.bfloat16)
-        for d in range(1, rows):
-            to_row(ch, d).start()
+        for k in range(rows - 1):
+            to_row(ch, 1 + lax.rem(k + 2 * row, rows - 1)).start()
         own(ch).start()
 
-    @pl.when(i >= 2 * delay)
+    @pl.when(i >= delay + LAG)
     def _():
-        hand_on(i - 2 * delay)
+        hand_on(i - delay - LAG)
 
     @pl.when(i == steps - 1)
     def _():
-        for ch in range(chunks - delay, chunks):
+        for ch in range(chunks - LAG, chunks):
             hand_on(ch)
 
         @pl.loop(0, chunks)

time: 71.4 us -> 72.2 us (1.011)
  Pallas kernels: 71.1 us -> 71.9 us
    pallas_call x1, Pallas kernels: 48.8 us -> 49.5 us  [channelize(): pl.pallas_call(kernel, grid=(steps,), out_shape=jax.ShapeDtypeStruct((pai...]
where the time goes in v4:
time: 72.2 us; the launch traced here: 71.9 us
  Pallas kernels  71.9 us (100%)
    pallas_call x1, Pallas kernels, channelize(): pl.pallas_call(kernel, grid=(steps,), out_shape=jax.ShapeDtypeStruct((pai...  49.5 us
    pallas_call x1, Pallas kernels, correlate(): pl.pallas_call(correlate_kernel, grid=(steps + 1,), out_shape=jax.ShapeDt...  22.4 us

profile of v4, /device:TPU:0, one launch (start us, length us, event | category | flops | bytes accessed | tf_op | source)
XLA Modules:
  0.0 71.9 jit_solution(4767917694975963505)
XLA Ops:
  0.0 49.5 %channelize.1.spectra = bf16[4,8,2,128,128]{4,3,2,1,0:T(8,128)(2,1)} custom-call(bf16[128,161792]{1,0:T(8,128)(2,1)} %refs_7_.1, bf16[128,161792]{1,0:T(8,128)(2,1)} %refs_7_.1, bf16[128,161792]{1,0:T(8,128)(2,1)} %refs_7_.1, bf16[128,161792]{1,0:T(8,128)(2,1)} %refs_7_.1, bf16[128,161792]{1,0:T(8,128)(2,1)} %refs_7_.1, bf16[128,161792]{1,0:T(8,128)(2,1)} %refs_7_.1, ...), custom_call_target="tpu_custom_call" | custom-call | tf_op jit(solution)/shard_map/channelize/pallas_call | solution.py:299
  49.6 22.4 %correlate.1 = bf16[4,32768,128]{2,1,0:T(8,128)(2,1)} custom-call(bf16[4,8,2,128,128]{4,3,2,1,0:T(8,128)(2,1)} %channelize.1.spectra), custom_call_target="tpu_custom_call" | custom-call | tf_op jit(solution)/shard_map/correlate/pallas_call | solution.py:394

commit v5 on v4

--- a/solution.py
+++ b/solution.py
@@ -16,8 +16,8 @@
 LANES = 128
 STEP = 8
 GROUP = 2
-LAG = 3
-MXU = 256
+LAG = 2
+WIDTH = 512
 PITCH = 17
 MESH = pl.DeviceIdType.MESH
 
@@ -208,16 +208,16 @@
     fold(0)
     for first in range(0, STEP, GROUP):
         span = slice(first * feed_dev, (first + GROUP) * feed_dev)
-        for q in range(TAPS * chans // MXU):
-            cols = slice(q * MXU, (q + 1) * MXU)
+        for q in range(TAPS * chans // WIDTH):
+            cols = slice(q * WIDTH, (q + 1) * WIDTH)
             ge = jnp.dot(even[span], even_w[:, cols], preferred_element_type=jnp.float32)
             go = jnp.dot(odd[span], odd_w[:, cols], preferred_element_type=jnp.float32)
             if q == 0 and first + GROUP < STEP:
                 fold(first + GROUP)
             low = ge + go
             high = ge - go
-            for t in range(MXU // LANES):
-                j = q * (MXU // LANES) + t
+            for t in range(WIDTH // LANES):
+                j = q * (WIDTH // LANES) + t
                 cut = slice(t * LANES, (t + 1) * LANES)
                 at = pl.ds(i * STEP + STEP - 2 - 2 * j + first, GROUP)
                 low_acc[at] += low[:, cut].reshape(GROUP, feed_dev, LANES)
@@ -251,8 +251,8 @@
                 stage[pl.ds(s + e, chans, stride=2 * STEP), :] = gain_re * re - gain_im * im
                 stage[pl.ds(STEP + s + e, chans, stride=2 * STEP), :] = gain_re * im + gain_im * re
         ready[ch] = stage[...].reshape(chans, 2 * STEP, LANES).astype(jnp.bfloat16)
-        for k in range(rows - 1):
-            to_row(ch, 1 + lax.rem(k + 2 * row, rows - 1)).start()
+        for d in range(1, rows):
+            to_row(ch, d).start()
         own(ch).start()
 
     @pl.when(i >= delay + LAG)
@@ -344,7 +344,7 @@
     jblocks = rows * cols // lax.axis_size("col")
     iblocks = iblock // feed_dev
     col = lax.axis_index("col")
-    wide = MXU // LANES
+    wide = WIDTH // LANES
 
     lefts = []
     for b in range(iblocks):

time: 72.2 us -> 71.1 us (0.985)
  Pallas kernels: 71.9 us -> 70.8 us
    pallas_call x1, Pallas kernels: 22.4 us -> 21.5 us  [correlate(): pl.pallas_call(correlate_kernel, grid=(steps + 1,), out_shape=jax.ShapeDt...]
where the time goes in v5:
time: 71.1 us; the launch traced here: 70.8 us
  Pallas kernels  70.8 us (100%)
    pallas_call x1, Pallas kernels, channelize(): pl.pallas_call(kernel, grid=(steps,), out_shape=jax.ShapeDtypeStruct((pai...  49.3 us
    pallas_call x1, Pallas kernels, correlate(): pl.pallas_call(correlate_kernel, grid=(steps + 1,), out_shape=jax.ShapeDt...  21.5 us

profile of v5, /device:TPU:0, one launch (start us, length us, event | category | flops | bytes accessed | tf_op | source)
XLA Modules:
  0.0 70.8 jit_solution(5305788167529320879)
XLA Ops:
  0.0 49.3 %channelize.1.spectra = bf16[4,8,2,128,128]{4,3,2,1,0:T(8,128)(2,1)} custom-call(bf16[128,161792]{1,0:T(8,128)(2,1)} %refs_7_.1, bf16[128,161792]{1,0:T(8,128)(2,1)} %refs_7_.1, bf16[128,161792]{1,0:T(8,128)(2,1)} %refs_7_.1, bf16[128,161792]{1,0:T(8,128)(2,1)} %refs_7_.1, bf16[128,161792]{1,0:T(8,128)(2,1)} %refs_7_.1, bf16[128,161792]{1,0:T(8,128)(2,1)} %refs_7_.1, ...), custom_call_target="tpu_custom_call" | custom-call | tf_op jit(solution)/shard_map/channelize/pallas_call | solution.py:299
  49.3 21.5 %correlate.1 = bf16[4,32768,128]{2,1,0:T(8,128)(2,1)} custom-call(bf16[4,8,2,128,128]{4,3,2,1,0:T(8,128)(2,1)} %channelize.1.spectra), custom_call_target="tpu_custom_call" | custom-call | tf_op jit(solution)/shard_map/correlate/pallas_call | solution.py:394
